TPU v7x, 32 devices: a whole 2x2x4 slice. The times are simulated.
32 devices in a mesh: grp: 2 (over y), col: 4 (over z), row: 2 (over x), sub: 2 (over core).
Axes of the slice: x: 2, y: 2, z: 4, core: 2. Of those that a mesh axis runs over, the one named last changes fastest.
Arguments:
- counts: int32 [8, 4], P(('grp', 'row', 'sub'), 'col'), parts along dimension 0, may hold values from 1 to 12, as said below
- point_x: int32 [8, 4, 1536], P(('grp', 'row', 'sub'), 'col'), parts along dimension 0, may hold values from 0 to 511
- point_y: int32 [8, 4, 1536], P(('grp', 'row', 'sub'), 'col'), parts along dimension 0, may hold values from 0 to 255
- point_rate: float32 [8, 4, 1536], P(('grp', 'row', 'sub'), 'col'), parts along dimension 0, may hold values from 0.003125 to 0.0234375
- point_amp: float32 [8, 4, 2, 1536], P(('grp', 'row', 'sub'), 'col'), parts along dimension 0, may hold values from -2 to 2
- prop_rate: float32 [1], replicated, may hold values from 0.003125 to 0.0234375
Outputs:
- hologram: float32 [2, 2048, 2048], P(None, ('grp', 'row', 'sub'), 'col'), parts along dimension 1
There are 2 independent parts, one for each index of `grp`. A program takes and returns all parts, laid end to end along the dimension named above; an argument that names none is the same for every part. Nothing has to cross between parts.
Inputs may be any that keep to these rules, and one draw needn't show every extreme that they name: Tile part (ty, tx) has counts[ty, tx] live blocks of 128 points; in every plane some tile part has all 12 blocks live.
All inputs are finite; a program needn't handle non-finite values.
Results may differ from a plain program's by a relative error of at most 0.0037.
Values sent between devices are 32-bit elements; how exact they have to be, the bound alone decides.
A program may use at most 64 MiB of HBM per device.

v0:
```python
import functools
import math

import jax
import jax.numpy as jnp
from jax import lax
from jax.experimental import pallas as pl
from jax.experimental.pallas import tpu as pltpu
from jax.sharding import PartitionSpec as P

HB = 64
BP = 128
T = 128
SLAB = 32
FIELDS = 8
BF = jnp.bfloat16
F32 = jnp.float32


def fitted(func, degree):
    import numpy as np

    nodes = 0.125 - 0.125 * np.cos(np.pi * (np.arange(64) + 0.5) / 64)
    return [float(v) for v in np.polynomial.Polynomial.fit(nodes, func(nodes), degree).convert().coef]


def cos_values(s):
    import numpy as np

    return np.cos(np.pi * np.sqrt(s))


def sin_values(s):
    import numpy as np

    return np.sinc(np.sqrt(s)) * np.pi


COS = fitted(cos_values, 3)
SIN = fitted(sin_values, 3)


def poly(coefs, s):
    value = jnp.full_like(s, coefs[-1])
    for c in coefs[-2::-1]:
        value = value * s + c
    return value


def turn(t):
    f = t - jnp.floor(t + 0.5)
    s = f * f
    c = poly(COS, s)
    n = f * poly(SIN, s)
    n2 = n + n
    return 1.0 - n2 * n, n2 * c


def gen_axis(first, rate, place, amp):
    lane = lax.broadcasted_iota(jnp.int32, (SLAB, BP), 0).astype(F32) + float(first)
    m = jnp.abs(lane - place) - HB
    re, im = turn(rate * (m * m))
    if amp is not None:
        re, im = amp[0] * re - amp[1] * im, amp[0] * im + amp[1] * re
    return lane, re, im


def fill(dst, tiles, col, params, sign_rows):
    rate, pos, amp = params
    k = jnp.floor(pos * (1.0 / T))
    place = pos - k * T
    count = len(tiles)
    need_hi = [(k == j).astype(F32).astype(BF) for j in tiles]
    need_lo = [(k == j - 1).astype(F32).astype(BF) for j in tiles]
    for first in range(0, T, SLAB):
        lane, re, im = gen_axis(first, rate, place, amp)
        above = lane >= place
        below = lane <= place
        hi_re = jnp.where(above, re, 0.0).astype(BF)
        hi_im = jnp.where(above, im, 0.0).astype(BF)
        lo_re = jnp.where(below, re, 0.0).astype(BF)
        lo_im = jnp.where(below, im, 0.0).astype(BF)
        for n, j in enumerate(tiles):
            if j == 0:
                t_re, t_im = hi_re * need_hi[n], hi_im * need_hi[n]
            else:
                t_re = hi_re * need_hi[n] + lo_re * need_lo[n]
                t_im = hi_im * need_hi[n] + lo_im * need_lo[n]
            row = n * T + first
            if sign_rows:
                im_row = count * T + row
                dst[row : row + SLAB, col : col + BP] = t_re
                dst[row : row + SLAB, col + BP : col + 2 * BP] = -t_im
                dst[im_row : im_row + SLAB, col : col + BP] = t_im
                dst[im_row : im_row + SLAB, col + BP : col + 2 * BP] = t_re
            else:
                dst[row : row + SLAB, col : col + BP] = t_re
                dst[row : row + SLAB, col + BP : col + 2 * BP] = t_im


def add_source(pts, row_tiles, col_tiles, dst_row, dst_col, chunk, left, right, acc):
    count = jnp.max(pts[5:6, :BP]).astype(jnp.int32)
    nr, nc = len(row_tiles), len(col_tiles)

    @pl.loop(0, (count + chunk - 1) // chunk)
    def _(step):
        for b in range(chunk):
            offset = pl.multiple_of((step * chunk + b) * BP, BP)
            x = pts[0:1, pl.ds(offset, BP)]
            y = pts[1:2, pl.ds(offset, BP)]
            rate = pts[2:3, pl.ds(offset, BP)] * (0.5 / math.pi)
            amp = (pts[3:4, pl.ds(offset, BP)], pts[4:5, pl.ds(offset, BP)])
            fill(left, row_tiles, 2 * BP * b, (rate, y, None), True)
            fill(right, col_tiles, 2 * BP * b, (rate, x, amp), False)
        product = lax.dot_general(
            left[: 2 * nr * T, : 2 * BP * chunk],
            right[: nc * T, : 2 * BP * chunk],
            (((1,), (1,)), ((), ())),
            preferred_element_type=F32,
        )
        rows = slice(dst_row * T, (dst_row + nr) * T)
        cols = slice(dst_col * T, (dst_col + nc) * T)
        acc[0, rows, cols] += product[: nr * T]
        acc[1, rows, cols] += product[nr * T :]


def split(value):
    high = value.astype(BF)
    return high, (value - high.astype(F32)).astype(BF)


def band(prop, in_dim):
    shape = (2 * T, T) if in_dim == 0 else (T, 2 * T)
    offset = (
        lax.broadcasted_iota(jnp.int32, shape, in_dim)
        - lax.broadcasted_iota(jnp.int32, shape, 1 - in_dim)
        - HB
    ).astype(F32)
    re, im = turn(prop * (0.5 / math.pi) * (offset * offset))
    inside = jnp.abs(offset) <= HB
    scale = 1.0 / math.sqrt(2 * HB + 1)
    return jnp.where(inside, re * scale, 0.0), jnp.where(inside, im * scale, 0.0)


def field_kernel(prop, own, near, out, left, right, acc, across):
    rows_n, cols_n = acc.shape[1] // T, acc.shape[2] // T
    acc[...] = jnp.zeros_like(acc)
    all_rows, all_cols = list(range(rows_n)), list(range(cols_n))
    add_source(own, all_rows, all_cols, 0, 0, 4, left, right, acc)
    pick_r = {-1: ([rows_n - 1], 0), 0: (all_rows, 0), 1: ([0], rows_n - 1)}
    pick_c = {-1: ([cols_n - 1], 0), 0: (all_cols, 0), 1: ([0], cols_n - 1)}
    for index, (dy, dx) in enumerate(SHIFTS):
        (row_tiles, dst_row), (col_tiles, dst_col) = pick_r[dy], pick_c[dx]
        add_source(near.at[index], row_tiles, col_tiles, dst_row, dst_col, 1, left, right, acc)

    _, at_row, n_row, at_col, n_col = position()
    edges = (at_row == 0, at_row == n_row - 1, at_col == 0, at_col == n_col - 1)
    ends = (
        (slice(0, HB), slice(None)),
        (slice(rows_n * T - HB, rows_n * T), slice(None)),
    )
    for e, (r, c) in enumerate(ends):

        @pl.when(edges[e])
        def _():
            acc[:, r, c] = jnp.zeros_like(acc[:, r, c])

    lanes = lax.broadcasted_iota(jnp.int32, (1, T), 1)
    for e, col, keep in ((2, 0, lanes >= HB), (3, (cols_n - 1) * T, lanes < T - HB)):

        @pl.when(edges[e])
        def _():
            acc[:, :, col : col + T] = jnp.where(keep[None], acc[:, :, col : col + T], 0.0)

    re, im = band(prop[0], 0)
    table = jnp.concatenate(
        [jnp.concatenate([re, im], 1), jnp.concatenate([-im, re], 1)], 0
    )
    tables = split(table)
    for j in range(cols_n - 1):
        cols = slice(j * T, (j + 2) * T)
        data = jnp.concatenate([acc[0, :, cols], acc[1, :, cols]], 1).astype(BF)
        result = sum(jnp.dot(data, t, preferred_element_type=F32) for t in tables)
        across[0, :, j * T : (j + 1) * T] = result[:, :T].astype(BF)
        across[1, :, j * T : (j + 1) * T] = result[:, T:].astype(BF)

    re, im = band(prop[0], 1)
    table = jnp.concatenate(
        [jnp.concatenate([re, -im], 1), jnp.concatenate([im, re], 1)], 0
    )
    tables = split(table)
    for q in range(rows_n - 1):
        rows = slice(q * T, (q + 2) * T)
        data = jnp.concatenate([across[0, rows, :], across[1, rows, :]], 0)
        result = sum(jnp.dot(t, data, preferred_element_type=F32) for t in tables)
        out[0, q * T : (q + 1) * T, :] = result[:T]
        out[1, q * T : (q + 1) * T, :] = result[T:]


SHIFTS = ((0, -1), (0, 1), (-1, 0), (1, 0), (-1, -1), (-1, 1), (1, -1), (1, 1))


def position():
    n_sub = lax.axis_size("sub")
    at_row = lax.axis_index("row") * n_sub + lax.axis_index("sub")
    return n_sub, at_row, lax.axis_size("row") * n_sub, lax.axis_index("col"), lax.axis_size("col")


def exchange_kernel(counts, px, py, pr, pa, own_out, near_out, own, near, send, recv):
    n_sub, at_row, n_row, at_col, n_col = position()

    def neighbour(dy, dx):
        y, x = at_row + dy, at_col + dx
        there = (y >= 0) & (y < n_row) & (x >= 0) & (x < n_col)
        return there, (lax.axis_index("grp"), x, lax.div(y, n_sub), lax.rem(y, n_sub))

    barrier = pltpu.get_barrier_semaphore()
    for shift in SHIFTS:
        there, device = neighbour(*shift)

        @pl.when(there)
        def _():
            pl.semaphore_signal(
                barrier, inc=1, device_id=device, device_id_type=pl.DeviceIdType.MESH
            )

    count = counts[0, 0]
    live = lax.broadcasted_iota(jnp.int32, px.shape, 1) < count * BP
    own[0:1] = px[...].astype(F32)
    own[1:2] = py[...].astype(F32)
    own[2:3] = pr[...]
    own[3:4] = jnp.where(live, pa[0:1], 0.0)
    own[4:5] = jnp.where(live, pa[1:2], 0.0)
    own[5:8] = jnp.broadcast_to(count.astype(F32), (3, px.shape[1]))
    own_out[...] = own[...]

    tall = 3 - (at_row == 0).astype(jnp.int32) - (at_row == n_row - 1).astype(jnp.int32)
    broad = 3 - (at_col == 0).astype(jnp.int32) - (at_col == n_col - 1).astype(jnp.int32)
    pl.semaphore_wait(barrier, tall * broad - 1)

    def copy(index, shift):
        there, device = neighbour(*shift)
        return there, pltpu.make_async_remote_copy(
            src_ref=own,
            dst_ref=near.at[index],
            send_sem=send.at[index],
            recv_sem=recv.at[index],
            device_id=device,
            device_id_type=pl.DeviceIdType.MESH,
        )

    back = [SHIFTS.index((-dy, -dx)) for dy, dx in SHIFTS]
    for index, shift in enumerate(SHIFTS):
        there, there_copy = copy(back[index], shift)

        @pl.when(there)
        def _():
            there_copy.start()

    for index, shift in enumerate(SHIFTS):
        there, _ = neighbour(*shift)
        _, incoming = copy(index, shift)

        @pl.when(there)
        def _():
            incoming.wait_recv()
            near_out[index] = near[index]

        @pl.when(jnp.logical_not(there))
        def _():
            near_out[index] = jnp.zeros_like(near_out[index])

    for index, shift in enumerate(SHIFTS):
        there, there_copy = copy(back[index], shift)

        @pl.when(there)
        def _():
            there_copy.wait_send()


def on_device(th, tw, counts, point_x, point_y, point_rate, point_amp, prop_rate):
    points = point_x.shape[-1]
    vmem = pl.BlockSpec(memory_space=pltpu.VMEM)
    smem = pl.BlockSpec(memory_space=pltpu.SMEM)
    own, near = pl.pallas_call(
        exchange_kernel,
        out_shape=[
            jax.ShapeDtypeStruct((FIELDS, points), F32),
            jax.ShapeDtypeStruct((len(SHIFTS), FIELDS, points), F32),
        ],
        in_specs=[smem, vmem, vmem, vmem, vmem],
        out_specs=[vmem, vmem],
        scratch_shapes=[
            pltpu.VMEM((FIELDS, points), F32),
            pltpu.VMEM((len(SHIFTS), FIELDS, points), F32),
            pltpu.SemaphoreType.DMA((len(SHIFTS),)),
            pltpu.SemaphoreType.DMA((len(SHIFTS),)),
        ],
        compiler_params=pltpu.CompilerParams(collective_id=0, has_side_effects=True),
    )(counts, point_x[0], point_y[0], point_rate[0], point_amp[0, 0])
    wide, high = tw + 2 * HB, th + 2 * HB
    return pl.pallas_call(
        field_kernel,
        out_shape=jax.ShapeDtypeStruct((2, th, tw), F32),
        in_specs=[smem, vmem, vmem],
        out_specs=vmem,
        scratch_shapes=[
            pltpu.VMEM((2 * high, 8 * BP), BF),
            pltpu.VMEM((wide, 8 * BP), BF),
            pltpu.VMEM((2, high, wide), F32),
            pltpu.VMEM((2, high, tw), BF),
        ],
        compiler_params=pltpu.CompilerParams(vmem_limit_bytes=48 * 1024 * 1024),
    )(prop_rate, own, near)


def solution(mesh):
    th, tw = 256, 512
    return jax.shard_map(
        functools.partial(on_device, th, tw),
        mesh=mesh,
        in_specs=(
            P(("grp", "row", "sub"), "col"),
            P(("grp", "row", "sub"), "col", None),
            P(("grp", "row", "sub"), "col", None),
            P(("grp", "row", "sub"), "col", None),
            P(("grp", "row", "sub"), "col", None, None),
            P(),
        ),
        out_specs=P(None, ("grp", "row", "sub"), "col"),
        check_vma=False,
    )
```

profile of v0, /device:TPU:10, one launch (start us, length us, event | category | flops | bytes accessed | tf_op | source)
XLA Modules:
  0.0 43.3 jit_solution(14530445607703045093)
XLA Ops:
  1.3 9.0 %shard_map.64 = (f32[8,1536]{1,0:T(8,128)}, f32[8,8,1536]{2,1,0:T(8,128)}) custom-call(s32[1,1]{1,0:T(1,128)S(6)} %copy.7.counts, s32[1,1536]{1,0:T(1,128)} %bitcast.5, s32[1,1536]{1,0:T(1,128)} %bitcast.6, f32[1,1536]{1,0:T(1,128)} %bitcast.7, f32[2,1536]{1,0:T(2,128)} %bitcast.4), custom_call_target="tpu_custom_call" | custom-call | tf_op jit(solution)/shard_map/pallas_call | solution.py:285
  10.3 0.0 copy-start
  10.3 1.0 %copy-done = f32[8,8,1536]{2,1,0:T(8,128)S(1)} copy-done((f32[8,8,1536]{2,1,0:T(8,128)S(1)}, f32[8,8,1536]{2,1,0:T(8,128)}, u32[]{:S(2)}) %copy-start) | copy-done | bytes 393240
  11.3 0.0 copy-start.1
  11.3 0.8 %copy-done.1 = f32[8,1536]{1,0:T(8,128)S(1)} copy-done((f32[8,1536]{1,0:T(8,128)S(1)}, f32[8,1536]{1,0:T(8,128)}, u32[]{:S(2)}) %copy-start.1) | copy-done | bytes 49176
  12.1 31.2 %shard_map.65 = f32[2,256,512]{2,1,0:T(8,128)} custom-call(f32[1]{0:T(128)S(6)} %copy.8.prop, f32[8,1536]{1,0:T(8,128)S(1)} %copy-done.1, f32[8,8,1536]{2,1,0:T(8,128)S(1)} %copy-done), custom_call_target="tpu_custom_call" | custom-call | tf_op jit(solution)/shard_map/pallas_call | solution.py:302
Async XLA Ops:
  10.3 1.0 %copy-start = (f32[8,8,1536]{2,1,0:T(8,128)S(1)}, f32[8,8,1536]{2,1,0:T(8,128)}, u32[]{:S(2)}) copy-start(f32[8,8,1536]{2,1,0:T(8,128)} %get-tuple-element.8.near) | copy-start | bytes 1179652
  11.3 0.8 %copy-start.1 = (f32[8,1536]{1,0:T(8,128)S(1)}, f32[8,1536]{1,0:T(8,128)}, u32[]{:S(2)}) copy-start(f32[8,1536]{1,0:T(8,128)} %get-tuple-element.7.own) | copy-start | bytes 147460
where the time goes:
time: 42.6 us; the launch traced here: 43.3 us
  Pallas kernels  40.2 us (94%)
  local copies, waits for them, and re-layouts  1.79 us (4%)
  between operations  1.31 us (3%)
    pallas_call x1, Pallas kernels, on_device(): pl.pallas_call(field_kernel, out_shape=jax.ShapeDtypeStruct((2, th, tw),...  31.2 us
    pallas_call x1, Pallas kernels, on_device(): pl.pallas_call(exchange_kernel, out_shape=[jax.ShapeDtypeStruct((FIELDS,...  9.01 us
    unnamed x4, local copies, waits for them, and re-layouts  1.79 us

commit v1 on v0

--- a/solution.py
+++ b/solution.py
@@ -98,18 +98,57 @@
                 dst[row : row + SLAB, col + BP : col + 2 * BP] = t_im
 
 
-def add_source(pts, row_tiles, col_tiles, dst_row, dst_col, chunk, left, right, acc):
-    count = jnp.max(pts[5:6, :BP]).astype(jnp.int32)
+def compact(near, packed, spans):
+    total = near.shape[2]
+    lane = lax.broadcasted_iota(jnp.int32, (len(SHIFTS), total), 1)
+    which = lax.broadcasted_iota(jnp.int32, (len(SHIFTS), total), 0)
+
+    def bound(pick):
+        value = jnp.zeros((len(SHIFTS), total), F32)
+        for i, span in enumerate(spans):
+            value = jnp.where(which == i, float(span[pick]), value)
+        return value
+
+    data = [near[:, f, :] for f in range(5)]
+    keep = lane.astype(F32) < near[:, 5, :] * float(BP)
+    keep = keep & (data[0] >= bound(0)) & (data[0] < bound(1))
+    keep = keep & (data[1] >= bound(2)) & (data[1] < bound(3))
+    flag = keep.astype(F32)
+    numbers = [jnp.sum(flag[i : i + 1]).astype(jnp.int32) for i in range(len(SHIFTS))]
+    gaps = jnp.where(keep, 0, 1)
+    step = 1
+    while step < total:
+        gaps = gaps + jnp.where(lane >= step, pltpu.roll(gaps, step, 1), 0)
+        step *= 2
+    move = jnp.where(keep, gaps, 0)
+    data = [jnp.where(keep, d, 0.0) for d in data]
+    step = 1
+    while step < total:
+        come = pltpu.roll(move, total - step, 1)
+        arrives = (come & step) != 0
+        leaves = (move & step) != 0
+        move = jnp.where(arrives, come, jnp.where(leaves, 0, move))
+        data = [
+            jnp.where(arrives, pltpu.roll(d, total - step, 1), jnp.where(leaves, 0.0, d))
+            for d in data
+        ]
+        step *= 2
+    for f in range(5):
+        packed[f] = data[f]
+    return numbers
+
+
+def add_source(pts, count, row_tiles, col_tiles, dst_row, dst_col, chunk, left, right, acc):
     nr, nc = len(row_tiles), len(col_tiles)
 
     @pl.loop(0, (count + chunk - 1) // chunk)
     def _(step):
         for b in range(chunk):
             offset = pl.multiple_of((step * chunk + b) * BP, BP)
-            x = pts[0:1, pl.ds(offset, BP)]
-            y = pts[1:2, pl.ds(offset, BP)]
-            rate = pts[2:3, pl.ds(offset, BP)] * (0.5 / math.pi)
-            amp = (pts[3:4, pl.ds(offset, BP)], pts[4:5, pl.ds(offset, BP)])
+            x = pts(0, offset)
+            y = pts(1, offset)
+            rate = pts(2, offset) * (0.5 / math.pi)
+            amp = (pts(3, offset), pts(4, offset))
             fill(left, row_tiles, 2 * BP * b, (rate, y, None), True)
             fill(right, col_tiles, 2 * BP * b, (rate, x, amp), False)
         product = lax.dot_general(
@@ -142,16 +181,30 @@
     return jnp.where(inside, re * scale, 0.0), jnp.where(inside, im * scale, 0.0)
 
 
-def field_kernel(prop, own, near, out, left, right, acc, across):
+def field_kernel(prop, own, near, out, left, right, acc, across, packed):
     rows_n, cols_n = acc.shape[1] // T, acc.shape[2] // T
     acc[...] = jnp.zeros_like(acc)
     all_rows, all_cols = list(range(rows_n)), list(range(cols_n))
-    add_source(own, all_rows, all_cols, 0, 0, 4, left, right, acc)
+    wide, high = float((cols_n - 1) * T), float((rows_n - 1) * T)
+    reach_c = {-1: (wide - T, wide), 0: (0.0, wide), 1: (0.0, float(T))}
+    reach_r = {-1: (high - T, high), 0: (0.0, high), 1: (0.0, float(T))}
+    numbers = compact(near, packed, [reach_c[dx] + reach_r[dy] for dy, dx in SHIFTS])
+
+    def own_points(f, offset):
+        return own[f : f + 1, pl.ds(offset, BP)]
+
+    count = jnp.max(own[5:6, :BP]).astype(jnp.int32)
+    add_source(own_points, count, all_rows, all_cols, 0, 0, 4, left, right, acc)
     pick_r = {-1: ([rows_n - 1], 0), 0: (all_rows, 0), 1: ([0], rows_n - 1)}
     pick_c = {-1: ([cols_n - 1], 0), 0: (all_cols, 0), 1: ([0], cols_n - 1)}
     for index, (dy, dx) in enumerate(SHIFTS):
         (row_tiles, dst_row), (col_tiles, dst_col) = pick_r[dy], pick_c[dx]
-        add_source(near.at[index], row_tiles, col_tiles, dst_row, dst_col, 1, left, right, acc)
+
+        def points(f, offset):
+            return packed[f, index : index + 1, pl.ds(offset, BP)]
+
+        blocks = (numbers[index] + BP - 1) // BP
+        add_source(points, blocks, row_tiles, col_tiles, dst_row, dst_col, 1, left, right, acc)
 
     _, at_row, n_row, at_col, n_col = position()
     edges = (at_row == 0, at_row == n_row - 1, at_col == 0, at_col == n_col - 1)
@@ -309,6 +362,7 @@
             pltpu.VMEM((wide, 8 * BP), BF),
             pltpu.VMEM((2, high, wide), F32),
             pltpu.VMEM((2, high, tw), BF),
+            pltpu.VMEM((5, len(SHIFTS), points), F32),
         ],
         compiler_params=pltpu.CompilerParams(vmem_limit_bytes=48 * 1024 * 1024),
     )(prop_rate, own, near)

time: 42.6 us -> 28.6 us (0.67)
  the two profiles are of different devices: /device:TPU:10 before, /device:TPU:13 now
where the time goes in v1:
time: 28.6 us; the launch traced here: 28.3 us
  Pallas kernels  25.2 us (88%)
  local copies, waits for them, and re-layouts  1.79 us (6%)
  between operations  1.31 us (5%)
    pallas_call x1, Pallas kernels, on_device(): pl.pallas_call(field_kernel, out_shape=jax.ShapeDtypeStruct((2, th, tw),...  16.4 us
    pallas_call x1, Pallas kernels, on_device(): pl.pallas_call(exchange_kernel, out_shape=[jax.ShapeDtypeStruct((FIELDS,...  8.87 us
    unnamed x4, local copies, waits for them, and re-layouts  1.79 us

profile of v1, /device:TPU:13, one launch (start us, length us, event | category | flops | bytes accessed | tf_op | source)
XLA Modules:
  0.0 28.3 jit_solution(13525456498020759129)
XLA Ops:
  1.3 8.9 %shard_map.64 = (f32[8,1536]{1,0:T(8,128)}, f32[8,8,1536]{2,1,0:T(8,128)}) custom-call(s32[1,1]{1,0:T(1,128)S(6)} %copy.7.counts, s32[1,1536]{1,0:T(1,128)} %bitcast.5, s32[1,1536]{1,0:T(1,128)} %bitcast.6, f32[1,1536]{1,0:T(1,128)} %bitcast.7, f32[2,1536]{1,0:T(2,128)} %bitcast.4), custom_call_target="tpu_custom_call" | custom-call | tf_op jit(solution)/shard_map/pallas_call | solution.py:338
  10.2 0.0 copy-start
  10.2 1.0 %copy-done = f32[8,8,1536]{2,1,0:T(8,128)S(1)} copy-done((f32[8,8,1536]{2,1,0:T(8,128)S(1)}, f32[8,8,1536]{2,1,0:T(8,128)}, u32[]{:S(2)}) %copy-start) | copy-done | bytes 393240
  11.2 0.0 copy-start.1
  11.2 0.8 %copy-done.1 = f32[8,1536]{1,0:T(8,128)S(1)} copy-done((f32[8,1536]{1,0:T(8,128)S(1)}, f32[8,1536]{1,0:T(8,128)}, u32[]{:S(2)}) %copy-start.1) | copy-done | bytes 49176
  12.0 16.4 %shard_map.65 = f32[2,256,512]{2,1,0:T(8,128)} custom-call(f32[1]{0:T(128)S(6)} %copy.8.prop, f32[8,1536]{1,0:T(8,128)S(1)} %copy-done.1, f32[8,8,1536]{2,1,0:T(8,128)S(1)} %copy-done), custom_call_target="tpu_custom_call" | custom-call | tf_op jit(solution)/shard_map/pallas_call | solution.py:355
Async XLA Ops:
  10.2 1.0 %copy-start = (f32[8,8,1536]{2,1,0:T(8,128)S(1)}, f32[8,8,1536]{2,1,0:T(8,128)}, u32[]{:S(2)}) copy-start(f32[8,8,1536]{2,1,0:T(8,128)} %get-tuple-element.8.near) | copy-start | bytes 1179652
  11.2 0.8 %copy-start.1 = (f32[8,1536]{1,0:T(8,128)S(1)}, f32[8,1536]{1,0:T(8,128)}, u32[]{:S(2)}) copy-start(f32[8,1536]{1,0:T(8,128)} %get-tuple-element.7.own) | copy-start | bytes 147460
